TPU v7x, 32 devices: a whole 2x2x4 slice. The times are simulated.
32 devices in a mesh: orb: 4 (over x, core), box: 8 (over z, y).
Axes of the slice: x: 2, y: 2, z: 4, core: 2. Of those that a mesh axis runs over, the one named last changes fastest.
Arguments:
- orbitals: bfloat16 [32, 48, 2304], P(('orb', 'box')), may hold values from -6 to 6
- corners: int32 [32, 3], replicated, may hold values from 0 to 8
- pairs: int32 [384, 2], P(('orb', 'box')), may hold values from 0 to 11, as said below
- counts: int32 [32], P(('orb', 'box')), may hold values from 1 to 12, as said below
Outputs:
- exchange: bfloat16 [32, 48, 2304], P(('orb', 'box'))
- gram: float32 [8, 4, 4], P('box')
Inputs may be any that keep to these rules, and one draw needn't show every extreme that they name: pairs[s, 0] is below 4 and pairs[s, 1] below 12; slots at or beyond their device's count are not used. `counts`: some device has all 12 slots live.
All inputs are finite; a program needn't handle non-finite values.
Results may differ from a plain program's by a relative error of at most 0.0049.
Values may be sent and summed in bfloat16 or wider, within the bound.
A program may use at most 192 MiB of HBM per device.

v0:
```python
import math

import jax
import jax.numpy as jnp
from jax import lax
from jax.sharding import PartitionSpec as P

SPAN = 8


screen_term = 0.5


def padded_2(cells, sides, width):
    for axis, dim in sides:
        count = lax.axis_size(axis)
        head = lax.slice_in_dim(cells, 0, width, axis=dim)
        tail = lax.slice_in_dim(cells, cells.shape[dim] - width, cells.shape[dim], axis=dim)
        cells = jnp.concatenate(
            [
                lax.ppermute(tail, axis, [(i, (i + 1) % count) for i in range(count)]),
                cells,
                lax.ppermute(head, axis, [((i + 1) % count, i) for i in range(count)]),
            ],
            axis=dim,
        )
    return cells


def from_behind(value, axis, steps):
    count = lax.axis_size(axis)
    pairs = [(source, (source + steps) % count) for source in range(count)]
    return lax.ppermute(value, axis, pairs)


def hartley_table(box_side):
    cell_index = jnp.arange(box_side, dtype=jnp.int32)
    phase = cell_index[:, None] * cell_index[None, :] % box_side
    angle = phase.astype(jnp.float32) * (2.0 * math.pi / box_side)
    return jnp.cos(angle) + jnp.sin(angle)


def green_table(box_side):
    cell_index = jnp.arange(box_side, dtype=jnp.int32)
    wave = jnp.minimum(cell_index, box_side - cell_index).astype(jnp.float32) * (
        2.0 * math.pi / box_side
    )
    squared_modulus = wave * wave
    total = (
        squared_modulus[:, None, None]
        + squared_modulus[None, :, None]
        + squared_modulus[None, None, :]
    )
    return 1.0 / (total + screen_term)


def transform(grid_values, cas_table):
    precision_high = lax.Precision.HIGHEST
    grid_values = jnp.einsum("am,mbc->abc", cas_table, grid_values, precision=precision_high)
    grid_values = jnp.einsum("bm,amc->abc", cas_table, grid_values, precision=precision_high)
    return jnp.einsum("cm,abm->abc", cas_table, grid_values, precision=precision_high)


def coulomb(density, cas_table, green_kernel):
    box_side = density.shape[0]
    spectrum = transform(density, cas_table) * green_kernel
    return transform(spectrum, cas_table) * (1.0 / box_side**3)


def place(grid_values, anchor):
    padded = jnp.pad(grid_values, SPAN)
    return lax.dynamic_slice(padded, (anchor[0], anchor[1], anchor[2]), grid_values.shape)


def add_cube(totals, position, update):
    current = lax.dynamic_index_in_dim(totals, position, 0, False)
    return lax.dynamic_update_index_in_dim(totals, current + update, position, 0)


def per_device(orbitals, corners, pairs, counts):
    box_side = orbitals.shape[1]
    plane_size = orbitals.shape[2]
    own_count = orbitals.shape[0]
    n_blocks = lax.axis_size("orb")
    n_regions = lax.axis_size("box")
    region_size = own_count * n_blocks
    box_index = lax.axis_index("box")
    block_index = lax.axis_index("orb")
    region_orbs = lax.all_gather(orbitals, "orb", axis=0, tiled=True)
    window_orbs = padded_2(region_orbs, (("box", 0),), region_size)
    cube_window = window_orbs.reshape(3 * region_size, box_side, box_side, box_side)
    positions = jnp.arange(3 * region_size, dtype=jnp.int32)
    section_of = positions // region_size
    member_of = positions % region_size
    neighbour = (box_index + section_of - 1 + n_regions) % n_regions
    global_ids = (
        member_of // own_count * n_regions + neighbour
    ) * own_count + member_of % own_count
    window_corners = jnp.take(corners, global_ids, axis=0)
    active = counts[0]
    cas_table = hartley_table(box_side)
    green_kernel = green_table(box_side)

    def one_pair(step, totals):
        leading_position = pairs[step, 0] + region_size
        second_pos = pairs[step, 1]
        phi_first = lax.dynamic_index_in_dim(cube_window, leading_position, 0, False).astype(
            jnp.float32
        )
        phi_second = lax.dynamic_index_in_dim(cube_window, second_pos, 0, False).astype(jnp.float32)
        offset = window_corners[second_pos] - window_corners[leading_position]
        second_here = place(phi_second, SPAN - offset)
        potential = coulomb(phi_first * second_here, cas_table, green_kernel)
        totals = add_cube(totals, leading_position, -potential * second_here)
        return add_cube(totals, second_pos, -place(potential * phi_first, SPAN + offset))

    totals = lax.fori_loop(
        0, active, one_pair, jnp.zeros((3 * region_size, box_side, box_side, box_side), jnp.float32)
    )
    from_above = from_behind(totals[:region_size].astype(jnp.bfloat16), "box", -1).astype(
        jnp.float32
    )
    from_below = from_behind(totals[2 * region_size :].astype(jnp.bfloat16), "box", 1).astype(
        jnp.float32
    )
    summed = totals[region_size : 2 * region_size] + from_above + from_below
    own_sums = lax.psum_scatter(
        summed.reshape(region_size, box_side, plane_size), "orb", scatter_dimension=0, tiled=True
    )
    own_cubes = own_sums.reshape(own_count, box_side, box_side, box_side)
    own_rows = block_index * own_count + jnp.arange(own_count, dtype=jnp.int32)

    def gram_entry(position):
        row_pos = position // own_count + region_size
        col_local = position % own_count
        col_pos = own_rows[col_local] + region_size
        offset = window_corners[row_pos] - window_corners[col_pos]
        row_cube = lax.dynamic_index_in_dim(cube_window, row_pos, 0, False).astype(jnp.float32)
        moved = place(row_cube, SPAN - offset)
        col_cube = lax.dynamic_index_in_dim(own_cubes, col_local, 0, False)
        return jnp.sum(moved * col_cube) / box_side**3

    columns = lax.map(gram_entry, jnp.arange(region_size * own_count, dtype=jnp.int32))
    columns = columns.reshape(region_size, own_count)
    gram_block = lax.all_gather(columns, "orb", axis=1, tiled=True)
    return (own_sums.astype(jnp.bfloat16), gram_block[None])


def solution(mesh):
    placed = (P(("orb", "box"), None, None), P(), P(("orb", "box"), None), P(("orb", "box")))
    return jax.shard_map(
        per_device,
        mesh=mesh,
        in_specs=placed,
        out_specs=(P(("orb", "box"), None, None), P("box", None, None)),
        check_vma=False,
    )
```

profile of v0, /device:TPU:0, one launch (start us, length us, event | category | flops | bytes accessed | tf_op | source)
XLA Modules:
  0.0 758.1 jit_solution(8290809457711760220)
XLA Ops:
  7.2 10.8 %all_gather.6 = bf16[4,48,2304]{2,1,0:T(8,128)(2,1)S(1)} all-gather(bf16[1,48,2304]{2,1,0:T(8,128)(2,1)} %param.8), channel_id=1, replica_groups=mesh['orb'=4,'box'=8] {'orb'}, dimensions={0}, use_global_device_ids=true | all-gather | bytes 1105920 | tf_op jit(solution)/shard_map/all_gather | solution.py:89
  18.0 4.6 collective-permute-start.1
  24.8 34.1 %collective-permute-done.1 = bf16[4,48,2304]{2,1,0:T(8,128)(2,1)S(1)} collective-permute-done((bf16[4,48,2304]{2,1,0:T(8,128)(2,1)S(1)}, bf16[4,48,2304]{2,1,0:T(8,128)(2,1)S(1)}, u32[]{:S(2)}, u32[]{:S(2)}) %collective-permute-start.1) | collective-permute-done | bytes 884768 | tf_op jit(solution)/shard_map/ppermute | solution.py:23
  61.5 10.7 %reshape.226 = bf16[12,48,48,48]{3,2,1,0:T(8,128)(2,1)} reshape(bf16[12,48,2304]{2,1,0:T(8,128)(2,1)S(1)} %pad_maximum_fusion) | data formatting | bytes 5308416 | tf_op jit(solution)/shard_map/reshape | solution.py:91
  72.2 6.4 broadcast_in_dim.42
  78.6 490.8 %while.28 = (s32[]{:T(128)}, f32[12,48,48,48]{3,2,1,0:T(8,128)}, s32[]{:T(128)}, s32[12,2]{0,1:T(2,128)S(1)}, bf16[12,48,48,48]{3,2,1,0:T(8,128)(2,1)}, /*index=...) while((s32[]{:T(128)}, f32[12,48,48,48]{3,2,1,0:T(8,128)}, ...), condition=%wide.region_1.2_spmd.clone.clone, body=%wide.region_0.1_spmd.clone.clone.sunk | while | flops 384113696 | bytes 15198023 | solution.py:117
  106.9 4.2 convolution_bitcast_fusion.11
  147.7 4.2 convolution_bitcast_fusion.11
  188.5 4.2 convolution_bitcast_fusion.11
  229.3 4.2 convolution_bitcast_fusion.11
  270.2 4.2 convolution_bitcast_fusion.11
  311.0 4.2 convolution_bitcast_fusion.11
  351.8 4.2 convolution_bitcast_fusion.11
  392.6 4.2 convolution_bitcast_fusion.11
  433.4 4.2 convolution_bitcast_fusion.11
  474.2 4.2 convolution_bitcast_fusion.11
  555.8 4.2 convolution_bitcast_fusion.11
  569.4 9.2 %convert.11 = bf16[12,48,48,48]{3,2,1,0:T(8,128)(2,1)} convert(f32[12,48,48,48]{3,2,1,0:T(8,128)} %get-tuple-element.260) | non-fusion elementwise | flops 1327104 | bytes 7962624 | tf_op jit(solution)/shard_map/convert.8
  584.0 77.4 %collective-permute-done.2 = bf16[4,48,48,48]{3,2,1,0:T(8,128)(2,1)S(1)} collective-permute-done((bf16[4,48,48,48]{3,2,1,0:T(8,128)(2,1)S(1)}, bf16[4,48,48,48]{3,2,1,0:T(8,128)(2,1)S(1)}, u32[]{:S(2)}, u32[]{:S(2)}) %collective-permute-start.2) | collective-permute-done | bytes 884768 | tf_op jit(solution)/shard_map/ppermute | solution.py:33
  661.3 5.3 convert_add_fusion
  666.6 5.2 reshape.227
  672.0 25.3 %reduce-scatter.2.cloned.1.call-done = f32[1,48,2304]{2,1,0:T(8,128)} async-done(((f32[4,48,2304]{2,1,0:T(8,128)}), f32[1,48,2304]{2,1,0:T(8,128)}) %reduce-scatter.2.cloned.1.call-update) | async-done | bytes 442384 | tf_op jit(solution)/shard_map/reduce_scatter | solution.py:127
  699.0 45.8 %while.27 = (s32[]{:T(128)}, f32[4]{0:T(128)S(1)}, s32[4]{0:T(128)S(1)}, bf16[12,48,48,48]{3,2,1,0:T(8,128)(2,1)}, s32[12,3]{0,1:T(4,128)S(1)}, /*index=5*/s32[1...) while((s32[]{:T(128)}, f32[4]{0:T(128)S(1)}, ...), condition=%wide.region_5.6_spmd, body=%wide.region_3.5_spmd.sunk | while | flops 331797 | bytes 1106321 | solution.py:143
  744.8 5.0 all-gather
  (250 shorter events, 299.1 us)
Async XLA Ops:
  7.2 690.1 %reduce-scatter.2.cloned.1.call-start = ((), (), s32[]{:S(2)}) async-start(), calls=%async_computation.1 | async-start | bytes 2211840 | tf_op jit(solution)/shard_map/reduce_scatter | solution.py:127
  18.0 40.9 %collective-permute-start.1 = (bf16[4,48,2304]{2,1,0:T(8,128)(2,1)S(1)}, bf16[4,48,2304]{2,1,0:T(8,128)(2,1)S(1)}, u32[]{:S(2)}, u32[]{:S(2)}) collective-permute-start(bf16[4,48,2304]{2,1,0:T(8,128)(2,1)S(1)} %all_gather.6), channel_id=1, source_target_pairs={{1,0},{2,1},{3,2},{4,3},{5,4},{6,5},{7,6},{0,7},{9,8},{10,9},{11,1... | collective-permute-start | bytes 2654216 | tf_op jit(solution)/shard_map/ppermute | solution.py:23
  22.6 37.2 %collective-permute-start = (bf16[4,48,2304]{2,1,0:T(8,128)(2,1)S(1)}, bf16[4,48,2304]{2,1,0:T(8,128)(2,1)}, u32[]{:S(2)}, u32[]{:S(2)}) collective-permute-start(bf16[4,48,2304]{2,1,0:T(8,128)(2,1)S(1)} %all_gather.6), channel_id=1, source_target_pairs={{0,1},{1,2},{2,3},{3,4},{4,5},{5,6},{6,7},{7,0},{8,9},{9,10},{10,1... | collective-permute-start | bytes 2654216 | tf_op jit(solution)/shard_map/ppermute | solution.py:21
  58.9 0.9 copy-start.1
  72.2 6.4 copy-start.2
  72.2 6.4 copy-start.3
  581.9 79.5 %collective-permute-start.2 = (bf16[4,48,48,48]{3,2,1,0:T(8,128)(2,1)S(1)}, bf16[4,48,48,48]{3,2,1,0:T(8,128)(2,1)S(1)}, u32[]{:S(2)}, u32[]{:S(2)}) collective-permute-start(bf16[4,48,48,48]{3,2,1,0:T(8,128)(2,1)S(1)} %get-tuple-element.387), channel_id=1, source_target_pairs={{0,7},{1,0},{2,1},{3,2},{4,3},{5,4},{6,5},{7,6},{8,15},{9,8},{10,9... | collective-permute-start | bytes 2654216 | tf_op jit(solution)/shard_map/ppermute | solution.py:33
  581.9 79.4 %collective-permute-start.3 = (bf16[4,48,48,48]{3,2,1,0:T(8,128)(2,1)S(1)}, bf16[4,48,48,48]{3,2,1,0:T(8,128)(2,1)S(1)}, u32[]{:S(2)}, u32[]{:S(2)}) collective-permute-start(bf16[4,48,48,48]{3,2,1,0:T(8,128)(2,1)S(1)} %get-tuple-element.388), channel_id=1, source_target_pairs={{0,1},{1,2},{2,3},{3,4},{4,5},{5,6},{6,7},{7,0},{8,9},{9,10},{10,1... | collective-permute-start | bytes 2654216 | tf_op jit(solution)/shard_map/ppermute | solution.py:33
  699.0 51.5 %copy-start = (f32[1,48,2304]{2,1,0:T(8,128)S(1)}, f32[1,48,2304]{2,1,0:T(8,128)}, u32[]{:S(2)}) copy-start(f32[1,48,2304]{2,1,0:T(8,128)} %reduce-scatter.2.cloned.1.call-done) | copy-start | bytes 1327108
Sparse Core Ops, SparseCore 0:
  672.0 25.2 reduce-scatter.1
where the time goes:
time: 757 us; the launch traced here: 758 us
  loops' own time  205 us (27%)
  matrix products  178 us (24%)
  waiting for transfers between devices  137 us (18%)
  local copies, waits for them, and re-layouts  118 us (16%)
  other arithmetic  83.7 us (11%)
  blocking collectives  15.8 us (2%)
  between operations  14.1 us (2%)
    another operation x1, loops' own time, per_device(): lax.fori_loop(0, active, one_pair, jnp.zeros((3 * region_size, box_side,...  175 us
    ppermute x2, waiting for transfers between devices, from_behind(): return lax.ppermute(value, axis, pairs)  77.4 us
    dot_general x24, matrix products, transform(): jnp.einsum('bm,amc->abc', cas_table, grid_values, precision=precision_high)  64.5 us
    dot_general x24, matrix products, transform(): jnp.einsum('cm,abm->abc', cas_table, grid_values, precision=precision_high)  60.1 us
    dot_general x24, matrix products, transform(): jnp.einsum('am,mbc->abc', cas_table, grid_values, precision=precision_high)  53.3 us
    ppermute x1, waiting for transfers between devices, padded_2(): lax.ppermute(head, axis, [((i + 1) % count, i) for i in range(count)])  34.1 us
    dynamic_slice x24, local copies, waits for them, and re-layouts, add_cube(): current = lax.dynamic_index_in_dim(totals, position, 0, False)  32.5 us
    another operation x1, loops' own time, per_device(): lax.map(gram_entry, jnp.arange(region_size * own_count, dtype=jnp.int32))  29.9 us
  transfers between devices with their start and end apart: 5, of which 3 were waited for; matrix products, arithmetic and copies ran while one was open for 0% of the time, Pallas kernels for 0%

commit v1 on v0

v1 whole, which is shorter than its diff:
```python
import functools
import math

import jax
import jax.numpy as jnp
import ml_dtypes
import numpy as np
from jax import lax
from jax.experimental import pallas as pl
from jax.experimental.pallas import tpu as pltpu
from jax.sharding import PartitionSpec as P

SPAN = 8
SCREEN = 0.5
HALF = 64
LANES = 128
STEP = 8
F32 = jnp.float32
BF16 = jnp.bfloat16


def tables(box):
    n = np.arange(box)
    angle = (n[:, None] * n[None, :] % box) * (2.0 * math.pi / box)
    cas = np.cos(angle) + np.sin(angle)
    hi = cas.astype(ml_dtypes.bfloat16)
    lo = (cas - hi.astype(np.float64)).astype(ml_dtypes.bfloat16)
    rows = np.concatenate([hi, hi, lo], axis=1)
    lanes = np.zeros((2 * LANES, 2 * LANES), ml_dtypes.bfloat16)
    for p in range(2):
        s = slice(HALF * p, HALF * p + box)
        t = slice(LANES + HALF * p, LANES + HALF * p + box)
        lanes[s, s] = hi
        lanes[t, s] = hi
        lanes[s, t] = lo
    k = np.minimum(n, box - n) * (2.0 * math.pi / box)
    k2 = k * k
    g = -1.0 / (k2[:, None, None] + k2[None, :, None] + k2[None, None, :] + SCREEN) / box**3
    green = np.zeros((box, box, LANES), np.float32)
    for p in range(2):
        green[:, :, HALF * p : HALF * p + box] = g
    return rows, lanes, green


def lane_ids(rows):
    return lax.broadcasted_iota(jnp.int32, (rows, LANES), 1)


def unpack_step(box, blocks, lane):
    out = []
    for t in range(STEP):
        start = box * t
        blk, off = start // LANES, start % LANES
        x = blocks[blk]
        if off + box > LANES:
            x = jnp.where(lane >= off, x, blocks[blk + 1])
        out.append((x, off))
    return out


def unpack_pair(box, first, second, lane):
    out = []
    for (x, off), (y, _) in zip(unpack_step(box, first, lane), unpack_step(box, second, lane)):
        a = pltpu.roll(x, (-off) % LANES, 1) if off else x
        b = pltpu.roll(y, (HALF - off) % LANES, 1) if off != HALF else y
        both = jnp.where(lane < HALF, a, b)
        out.append(jnp.where(lane % HALF < box, both, 0.0))
    return out


def pack_blocks(box, rows, shift, lane):
    n_blocks = box * STEP // LANES
    blocks = [None] * n_blocks
    for t in range(STEP):
        start = box * t
        amount = (start - shift) % LANES
        x = pltpu.roll(rows[t], amount, 1) if amount else rows[t]
        for blk in range(start // LANES, (start + box - 1) // LANES + 1):
            lo = start - blk * LANES
            if blocks[blk] is None:
                blocks[blk] = x
            else:
                blocks[blk] = jnp.where(lane >= max(lo, 0), x, blocks[blk])
    return blocks


def load_blocks(box, ref, lead, g):
    width = box * STEP
    start = pl.multiple_of(g * width, LANES)
    return [
        ref[(*lead, slice(None), pl.ds(start + LANES * k, LANES))].astype(F32)
        for k in range(width // LANES)
    ]


def split_rows(x):
    hi = x.astype(BF16)
    lo = (x - hi.astype(F32)).astype(BF16)
    return hi, lo


def row_transform(t_rows, xs):
    x = jnp.concatenate(xs, axis=1)
    hi, lo = split_rows(x)
    stacked = jnp.concatenate([hi, lo, hi], axis=0)
    y = jnp.dot(t_rows, stacked, preferred_element_type=F32)
    return y[:, :LANES], y[:, LANES:]


def lane_transform(t_lanes, x):
    hi, lo = split_rows(x)
    y = jnp.dot(jnp.concatenate([hi, lo], axis=1), t_lanes, preferred_element_type=F32)
    return y[:, :LANES] + y[:, LANES:]


def pair_kernel(
    dims, corners, pairs, counts, cubes, rows_ref, lanes_ref, green, out, held, acc, work, u_all, phi_all
):
    box, own, blocks, regions = dims
    region_size = own * blocks
    n_cubes = 3 * region_size
    box_index = lax.axis_index("box")
    lane = lane_ids(box)
    steps = box // STEP
    zero8 = jnp.zeros((SPAN, LANES), F32)

    def place_of(member, section):
        return (member // own) * (3 * own) + section * own + member % own

    def id_of(member, section):
        neighbour = lax.rem(box_index + section - 1 + regions, regions)
        return ((member // own) * regions + neighbour) * own + member % own

    def unpack(item, _):
        q, g = item // steps, item % steps
        first = load_blocks(box, cubes, (2 * q,), g)
        second = load_blocks(box, cubes, (2 * q + 1,), g)
        for t, row in enumerate(unpack_pair(box, first, second, lane)):
            b = g * STEP + t
            held[q, b, :SPAN] = zero8
            held[q, b, SPAN : SPAN + box] = row
            held[q, b, SPAN + box :] = zero8
            acc[q, b] = jnp.zeros((box + 2 * SPAN, LANES), F32)
        return 0

    lax.fori_loop(0, n_cubes // 2 * steps, unpack, 0)
    active = counts[0]

    def group(g, _):
        slots = []
        for p in range(2):
            slot = jnp.minimum(2 * g + p, active - 1)
            live = (2 * g + p < active).astype(F32)
            first, second = pairs[slot, 0], pairs[slot, 1]
            section = second // region_size
            member = second - section * region_size
            ci, cj = id_of(first, 1), id_of(member, section)
            e = [corners[cj, d] - corners[ci, d] for d in range(3)]
            i, j = place_of(first, 1), place_of(member, section)
            slots.append((live, i, j, e))

        def forward(c, _):
            rhos = []
            for t in range(STEP):
                b = c * STEP + t
                us, phis = [], []
                for p, (live, i, j, e) in enumerate(slots):
                    phi = pltpu.roll(held[i // 2, b, SPAN : SPAN + box], HALF * ((p + i) % 2), 1)
                    phis.append(phi * live)
                    bj = b - e[1]
                    inside = jnp.logical_and(bj >= 0, bj < box).astype(F32)
                    at = jnp.clip(bj, 0, box - 1)
                    u = held[j // 2, at, pl.ds(SPAN - e[0], box)]
                    amount = lax.rem(e[2] + HALF * (p + j % 2) + LANES, LANES)
                    us.append(pltpu.roll(u, amount, 1) * inside)
                u = jnp.where(lane < HALF, us[0], us[1])
                phi = jnp.where(lane < HALF, phis[0], phis[1])
                u_all[b] = u
                phi_all[b] = phi
                rhos.append(u * phi)
            y = lane_transform(lanes_ref[...], jnp.concatenate(rhos, axis=0))
            for t in range(0, STEP, 2):
                pair = row_transform(rows_ref[...], [y[box * t : box * (t + 1)], y[box * (t + 1) : box * (t + 2)]])
                start = pl.multiple_of((c * STEP + t) * box, 8)
                work[pl.ds(start, box)] = pair[0]
                work[pl.ds(start + box, box)] = pair[1]
            return 0

        lax.fori_loop(0, steps, forward, 0)

        def middle(c, _):
            for h in range(0, STEP, 2):
                a = c * STEP + h
                xs = [work[pl.ds(a + k, box, stride=box)] for k in range(2)]
                ys = row_transform(rows_ref[...], xs)
                zs = row_transform(rows_ref[...], [ys[k] * green[a + k] for k in range(2)])
                for k in range(2):
                    work[pl.ds(a + k, box, stride=box)] = zs[k]
            return 0

        lax.fori_loop(0, steps, middle, 0)

        def backward(c, _):
            xs = []
            for t in range(0, STEP, 2):
                start = pl.multiple_of((c * STEP + t) * box, 8)
                xs.extend(row_transform(rows_ref[...], [work[pl.ds(start, box)], work[pl.ds(start + box, box)]]))
            v_all = lane_transform(lanes_ref[...], jnp.concatenate(xs, axis=0))
            for t in range(STEP):
                b = c * STEP + t
                v = v_all[box * t : box * (t + 1)]
                vu = v * u_all[b]
                vp = v * phi_all[b]
                for p, (live, i, j, e) in enumerate(slots):
                    half = lane < HALF if p == 0 else lane >= HALF
                    acc[i // 2, b, SPAN : SPAN + box] += pltpu.roll(
                        jnp.where(half, vu, 0.0), HALF * ((p + i) % 2), 1
                    )
                    bj = b - e[1]
                    inside = jnp.logical_and(bj >= 0, bj < box).astype(F32)
                    at = jnp.clip(bj, 0, box - 1)
                    amount = lax.rem(HALF * (p + j % 2) + LANES - e[2], LANES)
                    acc[j // 2, at, pl.ds(SPAN - e[0], box)] += (
                        pltpu.roll(jnp.where(half, vp, 0.0), amount, 1) * inside
                    )
            return 0

        lax.fori_loop(0, steps, backward, 0)
        return 0

    lax.fori_loop(0, (active + 1) // 2, group, 0)

    def pack(item, _):
        q, g = item // steps, item % steps
        rows = [acc[q, g * STEP + t, SPAN : SPAN + box] for t in range(STEP)]
        start = pl.multiple_of(g * (box * STEP), LANES)
        for h in range(2):
            for k, block in enumerate(pack_blocks(box, rows, HALF * h, lane)):
                out[2 * q + h, :, pl.ds(start + LANES * k, LANES)] = block.astype(BF16)
        return 0

    lax.fori_loop(0, n_cubes // 2 * steps, pack, 0)


def gram_kernel(dims, corners, cubes, mid, above, below, exchange, gram, held):
    box, own, blocks, regions = dims
    region_size = own * blocks
    box_index, block_index = lax.axis_index("box"), lax.axis_index("orb")
    lane = lane_ids(box)
    steps = box // STEP
    zero8 = jnp.zeros((SPAN, LANES), F32)

    def id_of(member):
        return ((member // own) * regions + box_index) * own + member % own

    def unpack(item, _):
        q, g = item // steps, item % steps
        pieces = []
        for h in range(2):
            member = 2 * q + h
            pieces.append(load_blocks(box, cubes, (member // own, member % own), g))
        for t, row in enumerate(unpack_pair(box, pieces[0], pieces[1], lane)):
            b = g * STEP + t
            held[q, b, :SPAN] = zero8
            held[q, b, SPAN : SPAN + box] = row
            held[q, b, SPAN + box :] = zero8
        return 0

    lax.fori_loop(0, region_size // 2 * steps, unpack, 0)

    for col in range(own):
        me = id_of(block_index * own + col)
        shifts = []
        for k in range(region_size):
            ck = id_of(k)
            shifts.append([corners[ck, d] - corners[me, d] for d in range(3)])

        def step(g, sums):
            blocks_f = [
                a + b + c
                for a, b, c in zip(
                    load_blocks(box, mid, (col,), g),
                    load_blocks(box, above, (col,), g),
                    load_blocks(box, below, (col,), g),
                )
            ]
            start = pl.multiple_of(g * (box * STEP), LANES)
            for k, block in enumerate(blocks_f):
                exchange[col, :, pl.ds(start + LANES * k, LANES)] = block.astype(BF16)
            sums = list(sums)
            for t, (x, off) in enumerate(unpack_step(box, blocks_f, lane)):
                b = g * STEP + t
                x = pltpu.roll(x, (-off) % LANES, 1) if off else x
                x = jnp.where(lane < box, x, 0.0)
                for k in range(region_size):
                    e = shifts[k]
                    bj = b - e[1]
                    inside = jnp.logical_and(bj >= 0, bj < box).astype(F32)
                    at = jnp.clip(bj, 0, box - 1)
                    u = held[k // 2, at, pl.ds(SPAN - e[0], box)]
                    amount = lax.rem(e[2] + HALF * (k % 2) + LANES, LANES)
                    part = pltpu.roll(u, amount, 1) * x * inside
                    total = part[:8]
                    for r in range(8, box, 8):
                        total = total + part[r : r + 8]
                    sums[k] = sums[k] + total
            return tuple(sums)

        sums = lax.fori_loop(0, steps, step, tuple(jnp.zeros((8, LANES), F32) for _ in range(region_size)))
        for k in range(region_size):
            gram[k, col] = jnp.sum(sums[k]) * (1.0 / box**3)


def per_device(orbitals, corners, pairs, counts):
    own, box, plane = orbitals.shape
    blocks = lax.axis_size("orb")
    regions = lax.axis_size("box")
    region_size = own * blocks
    n_cubes = 3 * region_size
    dims = (box, own, blocks, regions)
    up = [(i, (i + 1) % regions) for i in range(regions)]
    down = [((i + 1) % regions, i) for i in range(regions)]
    mine = jnp.concatenate(
        [lax.ppermute(orbitals, "box", up), orbitals, lax.ppermute(orbitals, "box", down)], axis=0
    )
    gathered = lax.all_gather(mine, "orb", axis=0, tiled=True)
    rows, lanes, green = tables(box)
    smem = pl.BlockSpec(memory_space=pltpu.SMEM)
    vmem = pl.BlockSpec(memory_space=pltpu.VMEM)
    padded = (box, box + 2 * SPAN, LANES)
    totals = pl.pallas_call(
        functools.partial(pair_kernel, dims),
        out_shape=jax.ShapeDtypeStruct((n_cubes, box, plane), BF16),
        in_specs=[smem, smem, smem, vmem, vmem, vmem, vmem],
        out_specs=vmem,
        scratch_shapes=[
            pltpu.VMEM((n_cubes // 2, *padded), F32),
            pltpu.VMEM((n_cubes // 2, *padded), F32),
            pltpu.VMEM((box * box, LANES), F32),
            pltpu.VMEM((box, box, LANES), F32),
            pltpu.VMEM((box, box, LANES), F32),
        ],
        compiler_params=pltpu.CompilerParams(vmem_limit_bytes=60 * 2**20),
        name="pair_potentials",
    )(corners, pairs, counts, gathered, jnp.asarray(rows), jnp.asarray(lanes), jnp.asarray(green))
    reduced = lax.psum_scatter(totals, "orb", scatter_dimension=0, tiled=True)
    above = lax.ppermute(reduced[:own], "box", down)
    below = lax.ppermute(reduced[2 * own :], "box", up)
    region = gathered.reshape(blocks, 3, own, box, plane)[:, 1]
    exchange, columns = pl.pallas_call(
        functools.partial(gram_kernel, dims),
        out_shape=(
            jax.ShapeDtypeStruct((own, box, plane), BF16),
            jax.ShapeDtypeStruct((region_size, own), F32),
        ),
        in_specs=[smem, vmem, vmem, vmem, vmem],
        out_specs=(vmem, smem),
        scratch_shapes=[pltpu.VMEM((region_size // 2, *padded), F32)],
        compiler_params=pltpu.CompilerParams(vmem_limit_bytes=40 * 2**20),
        name="gram_columns",
    )(corners, region, reduced[own : 2 * own], above, below)
    gram = lax.all_gather(columns, "orb", axis=1, tiled=True)
    return exchange, gram[None]


def solution(mesh):
    placed = (P(("orb", "box"), None, None), P(), P(("orb", "box"), None), P(("orb", "box")))
    return jax.shard_map(
        per_device,
        mesh=mesh,
        in_specs=placed,
        out_specs=(P(("orb", "box"), None, None), P("box", None, None)),
        check_vma=False,
    )
```

time: 757 us -> 184 us (0.24)
  loops' own time: 205 us -> 0 us
  matrix products: 178 us -> 0 us
  local copies, waits for them, and re-layouts: 118 us -> 5.8 us
  other arithmetic: 83.7 us -> 1.97 us
  Pallas kernels: 0 us -> 26.7 us
  waiting for transfers between devices: 137 us -> 118 us
  blocking collectives: 15.8 us -> 5.03 us
    another operation x2 -> x0, loops' own time: 205 us -> none  [the longest x1 175 us: per_device(): lax.fori_loop(0, active, one_pair, jnp.zeros((3 * region_size, box_side,...]
    dot_general x72 -> x0, matrix products: 178 us -> none  [the longest x24 64.5 us: transform(): jnp.einsum('bm,amc->abc', cas_table, grid_values, precision=precision_high)]
    ppermute x4, waiting for transfers between devices: 111 us -> 17.1 us  [the longest x1 6.64 us: per_device(): lax.ppermute(orbitals, 'box', up)]
    reduce_scatter x1, waiting for transfers between devices: 25.3 us -> 78 us  [per_device(): reduced = lax.psum_scatter(totals, 'orb', scatter_dimension=0, tiled=True)]
    dynamic_slice x41 -> x0, local copies, waits for them, and re-layouts: 41.9 us -> none  [the longest x24 32.5 us: add_cube(): current = lax.dynamic_index_in_dim(totals, position, 0, False)]
    mul x25 -> x0, other arithmetic: 36.8 us -> none  [the longest x12 22.5 us: one_pair(): potential = coulomb(phi_first * second_here, cas_table, green_kernel)]
    pallas_call x0 -> x2, Pallas kernels: none -> 26.7 us  [the longest x1 21.7 us: per_device(): pl.pallas_call(functools.partial(pair_kernel, dims), out_shape=jax.ShapeD...]
    all_gather x0 -> x1, waiting for transfers between devices: none -> 22.5 us  [per_device(): gathered = lax.all_gather(mine, 'orb', axis=0, tiled=True)]
  transfers between devices with their start and end apart: 5 -> 6, of which waited for: 3 -> 6; matrix products, arithmetic and copies ran while one was open for 0% -> 2% of each run, Pallas kernels for 0% -> 0%
where the time goes in v1:
time: 184 us; the launch traced here: 182 us
  waiting for transfers between devices  118 us (64%)
  Pallas kernels  26.7 us (15%)
  between operations  14.7 us (8%)
  starting transfers between devices  10.5 us (6%)
  local copies, waits for them, and re-layouts  5.8 us (3%)
  blocking collectives  5.03 us (3%)
  other arithmetic  1.97 us (1%)
    reduce_scatter x1, waiting for transfers between devices, per_device(): reduced = lax.psum_scatter(totals, 'orb', scatter_dimension=0, tiled=True)  78 us
    all_gather x1, waiting for transfers between devices, per_device(): gathered = lax.all_gather(mine, 'orb', axis=0, tiled=True)  22.5 us
    pallas_call x1, Pallas kernels, per_device(): pl.pallas_call(functools.partial(pair_kernel, dims), out_shape=jax.ShapeD...  21.7 us
    ppermute x1, waiting for transfers between devices, per_device(): lax.ppermute(orbitals, 'box', up)  6.64 us
    all_gather x1, blocking collectives, per_device(): gram = lax.all_gather(columns, 'orb', axis=1, tiled=True)  5.03 us
    pallas_call x1, Pallas kernels, per_device(): pl.pallas_call(functools.partial(gram_kernel, dims), out_shape=(jax.Shape...  5.03 us
    ppermute x1, waiting for transfers between devices, per_device(): below = lax.ppermute(reduced[2 * own:], 'box', up)  4.9 us
    ppermute x1, starting transfers between devices, per_device(): above = lax.ppermute(reduced[:own], 'box', down)  4.29 us
  transfers between devices with their start and end apart: 6, of which 6 were waited for; matrix products, arithmetic and copies ran while one was open for 2% of the time, Pallas kernels for 0%

profile of v1, /device:TPU:0, one launch (start us, length us, event | category | flops | bytes accessed | tf_op | source)
XLA Modules:
  0.0 182.4 jit_solution(949205811386274924)
XLA Ops:
  7.2 0.0 all-gather.3.cloned.1.call-start
  7.2 3.0 %collective-permute-start = (bf16[1,48,2304]{2,1,0:T(8,128)(2,1)}, bf16[1,48,2304]{2,1,0:T(8,128)(2,1)S(1)}, u32[]{:S(2)}, u32[]{:S(2)}) collective-permute-start(bf16[1,48,2304]{2,1,0:T(8,128)(2,1)} %param.7), channel_id=1, source_target_pairs={{0,1},{1,2},{2,3},{3,4},{4,5},{5,6},{6,7},{7,0},{8,9},{9,10},{10,1... | collective-permute-start | bytes 663560 | tf_op jit(solution)/shard_map/ppermute | solution.py:324
  10.2 3.1 %collective-permute-start.1 = (bf16[1,48,2304]{2,1,0:T(8,128)(2,1)}, bf16[1,48,2304]{2,1,0:T(8,128)(2,1)S(1)}, u32[]{:S(2)}, u32[]{:S(2)}) collective-permute-start(bf16[1,48,2304]{2,1,0:T(8,128)(2,1)} %param.7), channel_id=1, source_target_pairs={{1,0},{2,1},{3,2},{4,3},{5,4},{6,5},{7,6},{0,7},{9,8},{10,9},{11,1... | collective-permute-start | bytes 663560 | tf_op jit(solution)/shard_map/ppermute | solution.py:324
  13.3 6.6 %collective-permute-done = bf16[1,48,2304]{2,1,0:T(8,128)(2,1)S(1)} collective-permute-done((bf16[1,48,2304]{2,1,0:T(8,128)(2,1)}, bf16[1,48,2304]{2,1,0:T(8,128)(2,1)S(1)}, u32[]{:S(2)}, u32[]{:S(2)}) %collective-permute-start) | collective-permute-done | bytes 221216 | tf_op jit(solution)/shard_map/ppermute | solution.py:324
  20.0 2.1 %collective-permute-done.1 = bf16[1,48,2304]{2,1,0:T(8,128)(2,1)S(1)} collective-permute-done((bf16[1,48,2304]{2,1,0:T(8,128)(2,1)}, bf16[1,48,2304]{2,1,0:T(8,128)(2,1)S(1)}, u32[]{:S(2)}, u32[]{:S(2)}) %collective-permute-start.1) | collective-permute-done | bytes 221216 | tf_op jit(solution)/shard_map/ppermute | solution.py:324
  22.1 1.9 %pad_maximum_fusion = bf16[3,48,2304]{2,1,0:T(8,128)(2,1)} fusion(bf16[1,48,2304]{2,1,0:T(8,128)(2,1)S(1)} %collective-permute-done.1, bf16[1,48,2304]{2,1,0:T(8,128)(2,1)} %param.7, bf16[1,48,2304]{2,1,0:T(8,128)(2,1)S(1)} %collective-permute-done), kind=kLoop, calls=%fused_computation.1 | loop fusion | flops 663552 | bytes 1327104 | tf_op jit(solution)/shard_map/concatenate | solution.py:323
  23.9 0.0 all-gather.3.cloned.1.call-update
  23.9 0.0 reduce-scatter.2.cloned.1.call-start
  24.0 1.4 copy.21.corners
  25.4 1.4 copy.20.pairs
  27.4 22.5 %all-gather.3.cloned.1.call-done.cubes = bf16[12,48,2304]{2,1,0:T(8,128)(2,1)} async-done(((bf16[3,48,2304]{2,1,0:T(8,128)(2,1)}), bf16[12,48,2304]{2,1,0:T(8,128)(2,1)}) %all-gather.3.cloned.1.call-update) | async-done | bytes 2654224 | tf_op jit(solution)/shard_map/all_gather | solution.py:326
  49.9 21.7 %pair_potentials.1 = bf16[12,48,2304]{2,1,0:T(8,128)(2,1)} custom-call(s32[32,3]{1,0:T(8,128)} %copy.21.corners, s32[12,2]{1,0:T(8,128)} %copy.20.pairs, s32[1]{0:T(128)S(6)} %copy.24.counts, bf16[12,48,2304]{2,1,0:T(8,128)(2,1)} %all-gather.3.cloned.1.call-done.cubes, bf16[48,144]{1,0:T(8,128)(2,1)} %constant.6.clone.rows_ref, ...), custom_call_target="tpu_custom_call" | custom-call | tf_op jit(solution)/shard_map/pair_potentials/pallas_call | solution.py:331
  71.6 0.0 reduce-scatter.2.cloned.1.call-update
  71.6 78.0 %reduce-scatter.2.cloned.1.call-done = bf16[3,48,2304]{2,1,0:T(8,128)(2,1)} async-done(((bf16[12,48,2304]{2,1,0:T(8,128)(2,1)}), bf16[3,48,2304]{2,1,0:T(8,128)(2,1)}) %reduce-scatter.2.cloned.1.call-update) | async-done | bytes 663568 | tf_op jit(solution)/shard_map/reduce_scatter | solution.py:346
  149.6 1.2 fusion
  150.8 4.3 %collective-permute-start.2 = (bf16[1,48,2304]{2,1,0:T(8,128)(2,1)S(1)}, bf16[1,48,2304]{2,1,0:T(8,128)(2,1)S(1)}, u32[]{:S(2)}, u32[]{:S(2)}) collective-permute-start(bf16[1,48,2304]{2,1,0:T(8,128)(2,1)S(1)} %get-tuple-element.7), channel_id=1, source_target_pairs={{1,0},{2,1},{3,2},{4,3},{5,4},{6,5},{7,6},{0,7},{9,8},{10,9},{11,1... | collective-permute-start | bytes 663560 | tf_op jit(solution)/shard_map/ppermute | solution.py:347
  155.1 0.0 collective-permute-start.3
  155.1 1.2 slice_bitcast_fusion.cubes
  156.4 3.5 %collective-permute-done.2.above = bf16[1,48,2304]{2,1,0:T(8,128)(2,1)S(1)} collective-permute-done((bf16[1,48,2304]{2,1,0:T(8,128)(2,1)S(1)}, bf16[1,48,2304]{2,1,0:T(8,128)(2,1)S(1)}, u32[]{:S(2)}, u32[]{:S(2)}) %collective-permute-start.2) | collective-permute-done | bytes 221216 | tf_op jit(solution)/shard_map/ppermute | solution.py:347
  159.8 4.9 %collective-permute-done.3.below = bf16[1,48,2304]{2,1,0:T(8,128)(2,1)S(1)} collective-permute-done((bf16[1,48,2304]{2,1,0:T(8,128)(2,1)S(1)}, bf16[1,48,2304]{2,1,0:T(8,128)(2,1)S(1)}, u32[]{:S(2)}, u32[]{:S(2)}) %collective-permute-start.3) | collective-permute-done | bytes 221216 | tf_op jit(solution)/shard_map/ppermute | solution.py:348
  164.7 5.0 %gram_columns.1 = (bf16[1,48,2304]{2,1,0:T(8,128)(2,1)}, f32[4,1]{1,0:T(4,128)S(1)}) custom-call(s32[32,3]{1,0:T(8,128)S(1)} %copy-done, bf16[4,1,48,2304]{3,2,1,0:T(8,128)(2,1)S(1)} %slice_bitcast_fusion.cubes, bf16[1,48,2304]{2,1,0:T(8,128)(2,1)S(1)} %get-tuple-element.8.mid, bf16[1,48,2304]{2,1,0:T(8,128)(2,1)S(1)} %collective-permute-done.2.above, ...), custom_call_target="tpu_custom_call" | custom-call | tf_op jit(solution)/shard_map/gram_columns/pallas_call | solution.py:350
  169.8 0.1 reduce
  169.9 5.0 %all-gather = f32[4,1,4]{2,1,0:T(1,128)S(1)} all-gather(f32[1,1,4]{2,1,0:T(1,128)S(1)} %bitcast.13), channel_id=1, replica_groups=mesh['orb'=4,'box'=8] {'orb'}, dimensions={0}, use_global_device_ids=true | all-gather | bytes 80 | tf_op jit(solution)/shard_map/all_gather | solution.py:362
  174.9 0.7 copy.22
  (2 shorter events, 0.0 us)
Async XLA Ops:
  7.2 42.7 %all-gather.3.cloned.1.call-start = ((), (), s32[]{:S(2)}) async-start(), calls=%async_computation.1 | async-start | bytes 3317760 | tf_op jit(solution)/shard_map/all_gather | solution.py:326
  7.2 12.8 %collective-permute-start = (bf16[1,48,2304]{2,1,0:T(8,128)(2,1)}, bf16[1,48,2304]{2,1,0:T(8,128)(2,1)S(1)}, u32[]{:S(2)}, u32[]{:S(2)}) collective-permute-start(bf16[1,48,2304]{2,1,0:T(8,128)(2,1)} %param.7), channel_id=1, source_target_pairs={{0,1},{1,2},{2,3},{3,4},{4,5},{5,6},{6,7},{7,0},{8,9},{9,10},{10,1... | collective-permute-start | bytes 663560 | tf_op jit(solution)/shard_map/ppermute | solution.py:324
  10.2 11.8 %collective-permute-start.1 = (bf16[1,48,2304]{2,1,0:T(8,128)(2,1)}, bf16[1,48,2304]{2,1,0:T(8,128)(2,1)S(1)}, u32[]{:S(2)}, u32[]{:S(2)}) collective-permute-start(bf16[1,48,2304]{2,1,0:T(8,128)(2,1)} %param.7), channel_id=1, source_target_pairs={{1,0},{2,1},{3,2},{4,3},{5,4},{6,5},{7,6},{0,7},{9,8},{10,9},{11,1... | collective-permute-start | bytes 663560 | tf_op jit(solution)/shard_map/ppermute | solution.py:324
  23.9 125.7 %reduce-scatter.2.cloned.1.call-start = ((), (), s32[]{:S(2)}) async-start(), calls=%async_computation.2 | async-start | bytes 3317760 | tf_op jit(solution)/shard_map/reduce_scatter | solution.py:346
  71.6 93.2 %copy-start = (s32[32,3]{1,0:T(8,128)S(1)}, s32[32,3]{1,0:T(8,128)}, u32[]{:S(2)}) copy-start(s32[32,3]{1,0:T(8,128)} %copy.21.corners) | copy-start | bytes 1156
  150.8 9.0 %collective-permute-start.2 = (bf16[1,48,2304]{2,1,0:T(8,128)(2,1)S(1)}, bf16[1,48,2304]{2,1,0:T(8,128)(2,1)S(1)}, u32[]{:S(2)}, u32[]{:S(2)}) collective-permute-start(bf16[1,48,2304]{2,1,0:T(8,128)(2,1)S(1)} %get-tuple-element.7), channel_id=1, source_target_pairs={{1,0},{2,1},{3,2},{4,3},{5,4},{6,5},{7,6},{0,7},{9,8},{10,9},{11,1... | collective-permute-start | bytes 663560 | tf_op jit(solution)/shard_map/ppermute | solution.py:347
  155.1 9.6 %collective-permute-start.3 = (bf16[1,48,2304]{2,1,0:T(8,128)(2,1)S(1)}, bf16[1,48,2304]{2,1,0:T(8,128)(2,1)S(1)}, u32[]{:S(2)}, u32[]{:S(2)}) collective-permute-start(bf16[1,48,2304]{2,1,0:T(8,128)(2,1)S(1)} %get-tuple-element.6), channel_id=1, source_target_pairs={{0,1},{1,2},{2,3},{3,4},{4,5},{5,6},{6,7},{7,0},{8,9},{9,10},{10,1... | collective-permute-start | bytes 663560 | tf_op jit(solution)/shard_map/ppermute | solution.py:348
Sparse Core Ops, SparseCore 0:
  24.1 25.7 all-gather.2
  71.7 77.8 reduce-scatter.1
